TPU v7x, 32 devices: a whole 2x2x4 slice. The times are simulated.
32 devices in a mesh: ctx: 4 (over y, x), tp: 8 (over z, core).
Axes of the slice: x: 2, y: 2, z: 4, core: 2. Of those that a mesh axis runs over, the one named last changes fastest.
Arguments:
- projected: bfloat16 [3, 1024, 6144], P(None, 'ctx', 'tp'), may hold values from -6 to 6
- filters: float32 [384, 128], P('tp'), may hold values from -0.5 to 0.5
- out_weight: bfloat16 [6144, 6144], P('tp'), may hold values from -0.109375 to 0.109375
- grad_out: bfloat16 [1024, 6144], P('ctx', 'tp'), may hold values from -6 to 6
Outputs:
- block_out: bfloat16 [1024, 6144], P('ctx', 'tp')
- grad_inputs: bfloat16 [3, 1024, 6144], P(None, 'ctx', 'tp')
- grad_weight: float32 [6144, 6144], P('tp', 'ctx')
- grad_filters: float32 [384, 128], P('tp', 'ctx')
All inputs are finite; a program needn't handle non-finite values.
Results may differ from a plain program's by a relative error of at most 0.0064.
Values may be sent and summed in bfloat16 or wider, within the bound.
A program may use at most 128 MiB of HBM per device.

v0:
```python
import functools
import math

import jax
import jax.numpy as jnp
from jax import lax
from jax.experimental import pallas as pl
from jax.experimental.pallas import tpu as pltpu
from jax.sharding import PartitionSpec as P

LANES = 128


def shifted(value, axis, steps):
    count = lax.axis_size(axis)
    first, last = (max(0, -steps), min(count, count - steps))
    return lax.ppermute(value, axis, [(source, source + steps) for source in range(first, last)])


def lane_group(rows, width, group_size):
    lane = lax.broadcasted_iota(jnp.int32, (rows, width), 1)
    return (lane % LANES) // group_size


def windows(extended, taps_count, blocks):
    return jnp.concatenate(
        [extended[b * taps_count : b * taps_count + 2 * taps_count] for b in range(blocks)], axis=1
    )


def toeplitz(row, taps_count, shift):
    spread = jnp.broadcast_to(row, (taps_count, 2 * taps_count))
    return pltpu.roll(spread, shift, 1, stride=1, stride_axis=0).astype(jnp.bfloat16)


def banded(table, shift, window, taps_count, group_size):
    width = window.shape[1]
    group = lane_group(taps_count, width, group_size)
    total = jnp.zeros((taps_count, width), jnp.float32)
    for g in range(LANES // group_size):
        tile = toeplitz(table[g : g + 1, :], taps_count, shift)
        part = jnp.dot(tile, window, preferred_element_type=jnp.float32)
        total = jnp.where(group == g, part, total)
    return total


def forward_kernel(group_size, taps_count, p_ref, halo_ref, table_ref, filtered_ref, mixed_ref):
    blocks = p_ref.shape[1] // taps_count
    gated = (p_ref[1].astype(jnp.float32) * p_ref[2].astype(jnp.float32)).astype(jnp.bfloat16)
    window = windows(jnp.concatenate([halo_ref[...], gated], axis=0), taps_count, blocks)
    total = banded(table_ref[...], 1, window, taps_count, group_size)
    for b in range(blocks):
        rows = slice(b * taps_count, (b + 1) * taps_count)
        part = total[:, b * LANES : (b + 1) * LANES]
        filtered_ref[rows, :] = part
        mixed_ref[rows, :] = (p_ref[0, rows, :].astype(jnp.float32) * part).astype(jnp.bfloat16)


def backward_kernel(
    group_size, taps_count, p_ref, halo_ref, next_ref, gm_ref, filtered_ref, table_ref, gi_ref, gt_ref
):
    blocks = p_ref.shape[1] // taps_count
    key, value = p_ref[1].astype(jnp.float32), p_ref[2].astype(jnp.float32)
    gated = (key * value).astype(jnp.bfloat16)
    grad_mixed = gm_ref[...]
    grad_filtered = (grad_mixed * p_ref[0].astype(jnp.float32)).astype(jnp.bfloat16)
    gi_ref[0] = (grad_mixed * filtered_ref[...]).astype(jnp.bfloat16)
    ahead = windows(jnp.concatenate([grad_filtered, next_ref[...]], axis=0), taps_count, blocks)
    total = banded(table_ref[...], 0, ahead, taps_count, group_size)
    for b in range(blocks):
        rows = slice(b * taps_count, (b + 1) * taps_count)
        part = total[:, b * LANES : (b + 1) * LANES]
        gi_ref[1, rows, :] = (part * value[rows]).astype(jnp.bfloat16)
        gi_ref[2, rows, :] = (part * key[rows]).astype(jnp.bfloat16)
    window = windows(jnp.concatenate([halo_ref[...], gated], axis=0), taps_count, blocks)
    width = blocks * LANES
    row = lax.broadcasted_iota(jnp.int32, (taps_count, taps_count), 0)
    col = lax.broadcasted_iota(jnp.int32, (taps_count, taps_count), 1)
    swap = (row + col == taps_count - 1).astype(jnp.float32).astype(jnp.bfloat16)
    reversed_rows = jnp.dot(swap, ahead[:taps_count], preferred_element_type=jnp.float32)
    group = lane_group(taps_count, width, group_size)
    for g in range(LANES // group_size):
        own = jnp.where(group == g, reversed_rows, 0.0).astype(jnp.bfloat16)
        product = lax.dot_general(
            own, window, (((1,), (1,)), ((), ())), preferred_element_type=jnp.float32
        )
        aligned = pltpu.roll(product, taps_count, 1, stride=1, stride_axis=0)
        gt_ref[g : g + 1, :] = jnp.sum(aligned, axis=0, keepdims=True)[:, :taps_count]


def local(projected, filters, out_weight, grad_out):
    out_rows = projected.shape[1]
    channels = projected.shape[2]
    groups, taps_count = filters.shape
    group_size = channels // groups
    tile_groups = LANES // group_size
    grid = (channels // LANES,)
    sequence = lax.axis_size("ctx") * out_rows
    taps = filters.astype(jnp.bfloat16).astype(jnp.float32)
    zeros = jnp.zeros_like(taps)
    table_ahead = jnp.concatenate([taps, zeros], axis=1)
    table_back = jnp.concatenate([taps[:, ::-1], zeros], axis=1)
    tail = projected[:, out_rows - taps_count :].astype(jnp.float32)
    earlier = shifted((tail[1] * tail[2]).astype(jnp.bfloat16), "ctx", 1)
    full_grad = lax.all_gather(grad_out, "tp", axis=1, tiled=True)

    p_spec = pl.BlockSpec((3, out_rows, LANES), lambda i: (0, 0, i))
    halo_spec = pl.BlockSpec((taps_count, LANES), lambda i: (0, i))
    row_spec = pl.BlockSpec((out_rows, LANES), lambda i: (0, i))
    table_spec = pl.BlockSpec((tile_groups, 2 * taps_count), lambda i: (i, 0))
    taps_spec = pl.BlockSpec((tile_groups, taps_count), lambda i: (i, 0))
    band_flops = 4 * channels * tile_groups * out_rows * taps_count
    vmem = pltpu.CompilerParams(vmem_limit_bytes=32 * 1024 * 1024)
    filtered, mixed = pl.pallas_call(
        functools.partial(forward_kernel, group_size, taps_count),
        grid=grid,
        in_specs=[p_spec, halo_spec, table_spec],
        out_specs=[row_spec, row_spec],
        out_shape=[
            jax.ShapeDtypeStruct((out_rows, channels), jnp.float32),
            jax.ShapeDtypeStruct((out_rows, channels), jnp.bfloat16),
        ],
        compiler_params=vmem,
        cost_estimate=pl.CostEstimate(
            flops=band_flops, bytes_accessed=out_rows * channels * 12, transcendentals=0
        ),
    )(projected, earlier, table_back)

    own_features = lax.psum_scatter(
        jnp.einsum("tc,cd->td", mixed, out_weight, preferred_element_type=jnp.float32),
        "tp",
        scatter_dimension=1,
        tiled=True,
    )
    block_out = own_features.astype(jnp.bfloat16)
    all_mixed = lax.all_gather(mixed, "ctx", axis=0, tiled=True)
    grad_mixed = jnp.einsum("td,cd->tc", full_grad, out_weight, preferred_element_type=jnp.float32)
    head = (grad_mixed[:taps_count] * projected[0, :taps_count].astype(jnp.float32)).astype(
        jnp.bfloat16
    )
    following = shifted(head, "ctx", -1)
    all_grad = lax.all_to_all(full_grad, "ctx", split_axis=1, concat_axis=0, tiled=True)
    grad_inputs, tap_grads = pl.pallas_call(
        functools.partial(backward_kernel, group_size, taps_count),
        grid=grid,
        in_specs=[p_spec, halo_spec, halo_spec, row_spec, row_spec, table_spec],
        out_specs=[p_spec, taps_spec],
        out_shape=[
            jax.ShapeDtypeStruct((3, out_rows, channels), jnp.bfloat16),
            jax.ShapeDtypeStruct((groups, taps_count), jnp.float32),
        ],
        compiler_params=vmem,
        cost_estimate=pl.CostEstimate(
            flops=2 * band_flops, bytes_accessed=out_rows * channels * 20, transcendentals=0
        ),
    )(projected, earlier, following, grad_mixed, filtered, table_ahead)
    filter_term = tap_grads[:, ::-1] / math.sqrt(sequence * group_size)
    grad_filters = lax.psum_scatter(filter_term, "ctx", scatter_dimension=1, tiled=True)
    grad_weight = jnp.einsum(
        "tc,td->cd", all_mixed, all_grad, preferred_element_type=jnp.float32
    ) * (1.0 / math.sqrt(sequence))
    return (block_out, grad_inputs, grad_weight, grad_filters)


def solution(mesh):
    placed = (P(None, "ctx", "tp"), P("tp", None), P("tp", None), P("ctx", "tp"))
    return jax.shard_map(
        local,
        mesh=mesh,
        in_specs=placed,
        out_specs=(P("ctx", "tp"), P(None, "ctx", "tp"), P("tp", "ctx"), P("tp", "ctx")),
        check_vma=False,
    )
```

profile of v0, /device:TPU:0, one launch (start us, length us, event | category | flops | bytes accessed | tf_op | source)
XLA Modules:
  0.0 211.2 jit_solution(4423931430611035928)
XLA Ops:
  7.2 0.0 all-gather.3.cloned.1.call-start
  7.2 2.0 copy.13
  9.3 0.0 all-gather.5.cloned.1.call-start
  9.3 1.2 slice_convert_fusion
  10.5 4.9 %collective-permute-start = (bf16[128,768]{1,0:T(8,128)(2,1)S(1)}, bf16[128,768]{1,0:T(8,128)(2,1)S(1)}, u32[]{:S(2)}, u32[]{:S(2)}) collective-permute-start(bf16[128,768]{1,0:T(8,128)(2,1)S(1)} %fusion.2), channel_id=1, source_target_pairs={{0,8},{8,16},{16,24},{1,9},{9,17},{17,25},{2,10},{10,18},{18,26},{... | collective-permute-start | bytes 589832 | tf_op jit(solution)/shard_map/ppermute | solution.py:17
  15.4 0.1 rev.6
  15.5 4.0 %collective-permute-done.halo_ref = bf16[128,768]{1,0:T(8,128)(2,1)S(1)} collective-permute-done((bf16[128,768]{1,0:T(8,128)(2,1)S(1)}, bf16[128,768]{1,0:T(8,128)(2,1)S(1)}, u32[]{:S(2)}, u32[]{:S(2)}) %collective-permute-start) | collective-permute-done | bytes 196640 | tf_op jit(solution)/shard_map/ppermute | solution.py:17
  19.5 3.6 %shard_map.75 = (f32[256,768]{1,0:T(8,128)S(1)}, bf16[256,768]{1,0:T(8,128)(2,1)}) custom-call(bf16[3,256,768]{2,1,0:T(8,128)(2,1)S(1)} %copy-done, bf16[128,768]{1,0:T(8,128)(2,1)S(1)} %collective-permute-done.halo_ref, f32[48,256]{1,0:T(8,128)S(1)} %concatenate.6.table_ref), custom_call_target="tpu_custom_call" | custom-call | flops 805306368 | bytes 2359296 | tf_op jit(solution)/shard_map/pallas_call | solution.py:114
  23.1 0.0 reduce-scatter.5.cloned.1.call-start
  23.1 9.1 %fusion.3 = f32[256,6144]{1,0:T(8,128)} fusion(bf16[256,768]{1,0:T(8,128)(2,1)} %get-tuple-element.8, bf16[768,6144]{1,0:T(8,128)(2,1)} %param.6), kind=kOutput, calls=%fused_computation.9 | convolution fusion | flops 2415919104 | bytes 16121856 | tf_op jit(solution)/shard_map/tc,cd->td/dot_general | solution.py:130
  32.3 19.0 %all-gather.3.cloned.1.call-done = bf16[256,6144]{0,1:T(8,128)(2,1)} async-done(((bf16[256,768]{0,1:T(8,128)(2,1)}), bf16[256,6144]{0,1:T(8,128)(2,1)}) %all-gather.3.cloned.1.call-update) | async-done | bytes 3145744 | tf_op jit(solution)/shard_map/all_gather | solution.py:105
  51.3 4.7 %all-to-all-start = ((bf16[256,4,1536]{0,2,1:T(8,128)(2,1)}), bf16[256,4,1536]{0,2,1:T(8,128)(2,1)}, u32[]{:S(2)}, u32[]{:S(2)}) async-start(bf16[256,4,1536]{0,2,1:T(8,128)(2,1)} %bitcast.17), calls=%async_computation.1 | async-start | bytes 6291456 | tf_op jit(solution)/shard_map/all_to_all | solution.py:142
  55.9 0.0 reduce-scatter.7.cloned.1.call-start
  56.0 7.6 %fusion.4.gm_ref = f32[256,768]{1,0:T(8,128)S(1)} fusion(bf16[256,6144]{0,1:T(8,128)(2,1)} %all-gather.3.cloned.1.call-done, bf16[768,6144]{1,0:T(8,128)(2,1)} %param.6), kind=kOutput, calls=%fused_computation.10 | convolution fusion | flops 2415919104 | bytes 13369344 | tf_op jit(solution)/shard_map/td,cd->tc/dot_general | solution.py:137
  63.6 1.3 collective-permute-start.1
  64.9 44.6 %collective-permute-done.1.next_ref = bf16[128,768]{1,0:T(8,128)(2,1)S(1)} collective-permute-done((bf16[128,768]{1,0:T(8,128)(2,1)S(1)}, bf16[128,768]{1,0:T(8,128)(2,1)S(1)}, u32[]{:S(2)}, u32[]{:S(2)}) %collective-permute-start.1) | collective-permute-done | bytes 196640 | tf_op jit(solution)/shard_map/ppermute | solution.py:17
  109.5 6.5 %shard_map.76 = (bf16[3,256,768]{2,1,0:T(8,128)(2,1)}, f32[48,128]{1,0:T(8,128)S(1)}) custom-call(bf16[3,256,768]{2,1,0:T(8,128)(2,1)S(1)} %copy-done, bf16[128,768]{1,0:T(8,128)(2,1)S(1)} %collective-permute-done.halo_ref, bf16[128,768]{1,0:T(8,128)(2,1)S(1)} %collective-permute-done.1.next_ref, f32[256,768]{1,0:T(8,128)S(1)} %fusion.4.gm_ref, ...), custom_call_target="tpu_custom_call" | custom-call | flops 1610612736 | bytes 3932160 | tf_op jit(solution)/shard_map/pallas_call | solution.py:143
  116.0 0.1 rev.7
  116.1 0.7 copy.16
  116.9 3.2 %copy.14 = bf16[4,256,1536]{2,1,0:T(8,128)(2,1)S(1)} copy(bf16[4,256,1536]{1,2,0:T(8,128)(2,1)} %bitcast.3) | data formatting | bytes 6291456 | tf_op jit(solution)/shard_map/all_to_all | solution.py:142
  120.1 5.7 %convolution_multiply_fusion = f32[768,1536]{1,0:T(8,128)} fusion(bf16[1024,768]{1,0:T(8,128)(2,1)} %all-gather.5.cloned.1.call-done, bf16[1024,1536]{1,0:T(8,128)(2,1)S(1)} %bitcast.16), kind=kOutput, calls=%fused_computation | convolution fusion | flops 2417098752 | bytes 9437184 | tf_op jit(solution)/shard_map/tc,td->cd/dot_general | solution.py:159
  125.8 53.6 %reduce-scatter.5.cloned.1.call-done = f32[256,768]{1,0:T(8,128)} async-done(((f32[256,6144]{1,0:T(8,128)}), f32[256,768]{1,0:T(8,128)}) %reduce-scatter.5.cloned.1.call-update) | async-done | bytes 786448 | tf_op jit(solution)/shard_map/reduce_scatter | solution.py:129
  179.4 1.9 convert_element_type.32
  181.4 23.3 %reduce-scatter.7.cloned.1.call-done = f32[32,48]{1,0:T(8,128)} async-done(((f32[128,48]{1,0:T(8,128)}), f32[32,48]{1,0:T(8,128)}) %reduce-scatter.7.cloned.1.call-update) | async-done | bytes 6160
  (16 shorter events, 0.2 us)
Async XLA Ops:
  7.2 12.3 %copy-start = (bf16[3,256,768]{2,1,0:T(8,128)(2,1)S(1)}, bf16[3,256,768]{2,1,0:T(8,128)(2,1)}, u32[]{:S(2)}) copy-start(bf16[3,256,768]{2,1,0:T(8,128)(2,1)} %p_ref.3) | copy-start | bytes 3538948
  7.2 8.2 %copy-start.1 = (f32[48,128]{1,0:T(8,128)S(1)}, f32[48,128]{1,0:T(8,128)}, u32[]{:S(2)}) copy-start(f32[48,128]{1,0:T(8,128)} %param.5) | copy-start | bytes 73732
  7.2 44.1 %all-gather.3.cloned.1.call-start = ((), (), s32[]{:S(2)}) async-start(), calls=%async_computation.4 | async-start | bytes 3538944 | tf_op jit(solution)/shard_map/all_gather | solution.py:105
  9.3 110.8 %all-gather.5.cloned.1.call-start = ((), (), s32[]{:S(2)}) async-start(), calls=%async_computation.5 | async-start | bytes 1966080 | tf_op jit(solution)/shard_map/all_gather | solution.py:136
  10.5 9.0 %collective-permute-start = (bf16[128,768]{1,0:T(8,128)(2,1)S(1)}, bf16[128,768]{1,0:T(8,128)(2,1)S(1)}, u32[]{:S(2)}, u32[]{:S(2)}) collective-permute-start(bf16[128,768]{1,0:T(8,128)(2,1)S(1)} %fusion.2), channel_id=1, source_target_pairs={{0,8},{8,16},{16,24},{1,9},{9,17},{17,25},{2,10},{10,18},{18,26},{... | collective-permute-start | bytes 589832 | tf_op jit(solution)/shard_map/ppermute | solution.py:17
  23.1 156.3 %reduce-scatter.5.cloned.1.call-start = ((), (), s32[]{:S(2)}) async-start(), calls=%async_computation.3 | async-start | bytes 7077888 | tf_op jit(solution)/shard_map/reduce_scatter | solution.py:129
  51.3 65.6 %all-to-all-start = ((bf16[256,4,1536]{0,2,1:T(8,128)(2,1)}), bf16[256,4,1536]{0,2,1:T(8,128)(2,1)}, u32[]{:S(2)}, u32[]{:S(2)}) async-start(bf16[256,4,1536]{0,2,1:T(8,128)(2,1)} %bitcast.17), calls=%async_computation.1 | async-start | bytes 6291456 | tf_op jit(solution)/shard_map/all_to_all | solution.py:142
  55.9 148.8 %reduce-scatter.7.cloned.1.call-start = ((), (), s32[]{:S(2)}) async-start(), calls=%async_computation.6 | async-start | bytes 81920
  63.6 45.9 %collective-permute-start.1 = (bf16[128,768]{1,0:T(8,128)(2,1)S(1)}, bf16[128,768]{1,0:T(8,128)(2,1)S(1)}, u32[]{:S(2)}, u32[]{:S(2)}) collective-permute-start(bf16[128,768]{1,0:T(8,128)(2,1)S(1)} %fusion), channel_id=1, source_target_pairs={{8,0},{16,8},{24,16},{9,1},{17,9},{25,17},{10,2},{18,10},{26,18},{... | collective-permute-start | bytes 589832 | tf_op jit(solution)/shard_map/ppermute | solution.py:17
Sparse Core Ops, SparseCore 0:
  10.2 40.9 all-gather.2
  53.7 53.6 all-gather.4
  109.7 69.7 reduce-scatter.4
  182.6 22.0 reduce-scatter.6
where the time goes:
time: 212 us; the launch traced here: 211 us
  waiting for transfers between devices  145 us (68%)
  matrix products  22.4 us (11%)
  between operations  13.9 us (7%)
  starting transfers between devices  11 us (5%)
  Pallas kernels  10.1 us (5%)
  local copies, waits for them, and re-layouts  6.08 us (3%)
  other arithmetic  3.17 us (1%)
    reduce_scatter x1, waiting for transfers between devices, local(): lax.psum_scatter(jnp.einsum('tc,cd->td', mixed, out_weight, preferred_ele...  53.6 us
    ppermute x2, waiting for transfers between devices, shifted(): lax.ppermute(value, axis, [(source, source + steps) for source in range(f...  48.6 us
    unnamed x5, waiting for transfers between devices  23.4 us
    all_gather x1, waiting for transfers between devices, local(): full_grad = lax.all_gather(grad_out, 'tp', axis=1, tiled=True)  19 us
    dot_general x1, matrix products, local(): jnp.einsum('tc,cd->td', mixed, out_weight, preferred_element_type=jnp.flo...  9.11 us
    dot_general x1, matrix products, local(): jnp.einsum('td,cd->tc', full_grad, out_weight, preferred_element_type=jnp...  7.56 us
    pallas_call x1, Pallas kernels, local(): pl.pallas_call(functools.partial(backward_kernel, group_size, taps_count)...  6.51 us
    ppermute x2, starting transfers between devices, shifted(): lax.ppermute(value, axis, [(source, source + steps) for source in range(f...  6.15 us
  transfers between devices with their start and end apart: 7, of which 5 were waited for; matrix products, arithmetic and copies ran while one was open for 14% of the time, Pallas kernels for 5%

commit v1 on v0

v1 whole, which is shorter than its diff:
```python
import functools
import math

import jax
import jax.numpy as jnp
from jax import lax
from jax.experimental import pallas as pl
from jax.experimental.pallas import tpu as pltpu
from jax.sharding import PartitionSpec as P

LANES = 128


def lane_group(rows, width, group_size):
    lane = lax.broadcasted_iota(jnp.int32, (rows, width), 1)
    return (lane % LANES) // group_size


def windows(extended, taps_count, blocks):
    return jnp.concatenate(
        [extended[b * taps_count : b * taps_count + 2 * taps_count] for b in range(blocks)], axis=1
    )


def toeplitz(row, taps_count, shift):
    spread = jnp.broadcast_to(row, (taps_count, 2 * taps_count))
    return pltpu.roll(spread, shift, 1, stride=1, stride_axis=0).astype(jnp.bfloat16)


def banded(table, shift, window, taps_count, group_size):
    width = window.shape[1]
    group = lane_group(taps_count, width, group_size)
    total = jnp.zeros((taps_count, width), jnp.float32)
    for g in range(LANES // group_size):
        tile = toeplitz(table[g : g + 1, :], taps_count, shift)
        part = jnp.dot(tile, window, preferred_element_type=jnp.float32)
        total = jnp.where(group == g, part, total)
    return total


def whole_kernel(
    ctx_size, tp_size, group_size, p_ref, table_back, table_ahead, w_ref, go_ref,
    block_ref, gi_ref, gw_ref, gt_ref,
    full, allg, allm, halo, following, filtered, gm, gf, part_out, part_in, mine, rs_out, rs_in,
    taps_own, taps_in,
    shift_sem, ag_send, ag_recv, mf_send, mf_recv, a2_send, a2_recv, am_send, am_recv,
    mix_send, mix_recv, pm_send, pm_recv, rs_send, rs_recv, tap_send, tap_recv,
):
    chips = tp_size // 2
    per = tp_size // ctx_size
    rows, channels = p_ref.shape[1], p_ref.shape[2]
    width = go_ref.shape[1]
    taps_count = halo.shape[0]
    blocks = rows // taps_count
    tile_groups = LANES // group_size
    sequence = ctx_size * rows
    ctx, tp = lax.axis_index("ctx"), lax.axis_index("tp")
    core, pos = lax.rem(tp, 2), lax.div(tp, 2)
    mate = tp + 1 - 2 * core
    f32, bf16 = jnp.float32, jnp.bfloat16

    def loop(first, last, step):
        def run(i, carry):
            step(i)
            return carry

        lax.fori_loop(first, last, run, 0)

    def remote(source, target, send, recv, c, t):
        return pltpu.make_async_remote_copy(
            src_ref=source, dst_ref=target, send_sem=send, recv_sem=recv,
            device_id=(c, t), device_id_type=pl.DeviceIdType.MESH,
        )

    def chip_after(d):
        return lax.rem(pos + d, chips) * 2 + core

    def chip_before(d):
        return lax.rem(pos - d + chips, chips) * 2 + core

    def ctx_after(d):
        return lax.rem(ctx + d, ctx_size)

    def ctx_before(d):
        return lax.rem(ctx - d + ctx_size, ctx_size)

    def lanes(i, size):
        return pl.ds(pl.multiple_of(i * size, LANES), size)

    barrier = pltpu.get_barrier_semaphore()

    def greet(c, t):
        pl.semaphore_signal(barrier, inc=1, device_id=(c, t), device_id_type=pl.DeviceIdType.MESH)

    loop(1, chips, lambda d: greet(ctx, chip_after(d)))
    loop(1, ctx_size, lambda d: greet(ctx_after(d), tp))
    greet(ctx, mate)
    pl.semaphore_wait(barrier, chips + ctx_size - 1)

    def ag_copy(d):
        return remote(go_ref, full.at[tp], ag_send.at[d], ag_recv.at[d], ctx, chip_after(d))

    def mate_copy(d):
        k = chip_before(d)
        return remote(full.at[k], full.at[k], mf_send.at[d], mf_recv.at[d], ctx, mate)

    def a2_copy(d):
        k = chip_before(d)
        owner, sub = lax.div(k, per), lax.rem(k, per)
        copy = remote(
            full.at[k], allg.at[ctx, sub], a2_send.at[d], a2_recv.at[ctx, sub], owner, tp
        )
        return owner != ctx, copy

    def start_a2(d):
        away, copy = a2_copy(d)

        @pl.when(away)
        def _():
            copy.start()

    halo_up = remote(gf.at[0:taps_count], halo, shift_sem.at[0], shift_sem.at[1], lax.rem(ctx + 1, ctx_size), tp)
    halo_down = remote(
        gf.at[0:taps_count], following, shift_sem.at[2], shift_sem.at[3], ctx_before(1), tp
    )
    has_next, has_last = ctx < ctx_size - 1, ctx > 0

    full[tp] = go_ref[...]
    tail = slice(rows - taps_count, rows)
    gf[0:taps_count, :] = (p_ref[1, tail, :].astype(f32) * p_ref[2, tail, :].astype(f32)).astype(bf16)

    @pl.when(has_next)
    def _():
        halo_up.start()

    loop(1, chips, lambda d: ag_copy(d).start())
    mate_copy(0).start()
    start_a2(0)

    @pl.when(has_last)
    def _():
        halo_up.wait_recv()

    @pl.when(jnp.logical_not(has_last))
    def _():
        halo[...] = jnp.zeros_like(halo)

    @pl.when(has_next)
    def _():
        halo_up.wait_send()

    def gated_window(i):
        at = lanes(i, LANES)
        gated = (p_ref[1, :, at].astype(f32) * p_ref[2, :, at].astype(f32)).astype(bf16)
        return windows(jnp.concatenate([halo[:, at], gated], axis=0), taps_count, blocks)

    def group_rows(i):
        return pl.ds(pl.multiple_of(i * tile_groups, tile_groups), tile_groups)

    def forward(i):
        at = lanes(i, LANES)
        total = banded(table_back[group_rows(i), :], 1, gated_window(i), taps_count, group_size)
        for b in range(blocks):
            span = slice(b * taps_count, (b + 1) * taps_count)
            part = total[:, b * LANES : (b + 1) * LANES]
            filtered[span, at] = part
            allm[ctx, span, at] = (p_ref[0, span, at].astype(f32) * part).astype(bf16)

    loop(0, channels // LANES, forward)

    def mix_copy(d):
        return remote(
            allm.at[ctx], allm.at[ctx], mix_send.at[d], mix_recv.at[d], ctx_after(d), tp
        )

    loop(1, ctx_size, lambda d: mix_copy(d).start())

    def pair_copy(m):
        return remote(part_out.at[m], part_in.at[m], pm_send.at[m], pm_recv.at[m], ctx, mate)

    def partial(k):
        return jnp.dot(allm[ctx], w_ref[:, lanes(k, width)], preferred_element_type=f32)

    def other_half(d):
        m = lax.rem(pos + d, chips)
        part_out[m] = partial(2 * m + 1 - core).astype(bf16)
        pair_copy(m).start()

    loop(1, chips + 1, other_half)

    def rs_copy(d):
        return remote(rs_out.at[d], rs_in.at[d], rs_send.at[d], rs_recv.at[d], ctx, chip_after(d))

    def own_half(d):
        k = chip_after(d)
        part = partial(k)
        pair_copy(lax.div(k, 2)).wait_recv()
        rs_out[d] = (part + part_in[lax.div(k, 2)].astype(f32)).astype(bf16)
        rs_copy(d).start()

    loop(1, chips, own_half)
    own_part = partial(tp)
    pair_copy(pos).wait_recv()
    mine[...] = own_part + part_in[pos].astype(f32)

    def add_grad(k):
        gm[...] += lax.dot_general(
            full[k], w_ref[:, lanes(k, width)], (((1,), (1,)), ((), ())),
            preferred_element_type=f32,
        )

    gm[...] = jnp.zeros_like(gm)
    add_grad(tp)

    def arrive(d):
        ag_copy(d).wait_recv()
        mate_copy(d).start()
        start_a2(d)
        add_grad(chip_before(d))

    def arrive_mate(d):
        mate_copy(d).wait_recv()
        add_grad(chip_before(d) + 1 - 2 * core)

    mate_first = 0
    arrive_mate(mate_first)
    loop(1, chips, arrive)
    loop(1, chips, arrive_mate)

    gf[...] = (gm[...] * p_ref[0].astype(f32)).astype(bf16)

    @pl.when(has_last)
    def _():
        halo_down.start()

    gi_ref[0] = (gm[...] * filtered[...]).astype(bf16)

    def relay_copy(source, sub):
        return remote(
            allg.at[source, sub], allg.at[source, sub], am_send.at[source, sub],
            am_recv.at[source, sub], ctx, mate,
        )

    def each_chunk(own, step):
        def outer(d):
            source = ctx_before(d)
            for sub in range(per):
                same = lax.rem(ctx * per + sub, 2) == core

                @pl.when(same if own else jnp.logical_not(same))
                def _():
                    step(source, sub)

        loop(1, ctx_size, outer)

    def relay(source, sub):
        remote(
            allg.at[source, sub], allg.at[source, sub], a2_send.at[0], a2_recv.at[source, sub], ctx, mate
        ).wait_recv()
        relay_copy(source, sub).start()

    each_chunk(True, relay)

    @pl.when(has_next)
    def _():
        halo_down.wait_recv()

    @pl.when(jnp.logical_not(has_next))
    def _():
        following[...] = jnp.zeros_like(following)

    row = lax.broadcasted_iota(jnp.int32, (taps_count, taps_count), 0)
    col = lax.broadcasted_iota(jnp.int32, (taps_count, taps_count), 1)
    swap = (row + col == taps_count - 1).astype(f32).astype(bf16)

    def backward(i):
        at = lanes(i, LANES)
        ahead = windows(
            jnp.concatenate([gf[:, at], following[:, at]], axis=0), taps_count, blocks
        )
        total = banded(table_ahead[group_rows(i), :], 0, ahead, taps_count, group_size)
        for b in range(blocks):
            span = slice(b * taps_count, (b + 1) * taps_count)
            part = total[:, b * LANES : (b + 1) * LANES]
            gi_ref[1, span, at] = (part * p_ref[2, span, at].astype(f32)).astype(bf16)
            gi_ref[2, span, at] = (part * p_ref[1, span, at].astype(f32)).astype(bf16)
        window = gated_window(i)
        reversed_rows = jnp.dot(swap, ahead[:taps_count], preferred_element_type=f32)
        group = lane_group(taps_count, blocks * LANES, group_size)
        found = []
        for g in range(tile_groups):
            own = jnp.where(group == g, reversed_rows, 0.0).astype(bf16)
            product = lax.dot_general(
                own, window, (((1,), (1,)), ((), ())), preferred_element_type=f32
            )
            aligned = pltpu.roll(product, taps_count, 1, stride=1, stride_axis=0)
            found.append(jnp.sum(aligned, axis=0, keepdims=True)[:, :taps_count])
        taps_own[group_rows(i), :] = jnp.concatenate(found, axis=0)

    loop(0, channels // LANES, backward)

    def tap_copy(d):
        return remote(taps_own, taps_in.at[d], tap_send.at[d], tap_recv.at[d], ctx_after(d), tp)

    loop(1, ctx_size, lambda d: tap_copy(d).start())

    each_chunk(False, lambda source, sub: relay_copy(source, sub).wait_recv())
    loop(1, ctx_size, lambda d: mix_copy(d).wait_recv())
    for sub in range(per):
        allg[ctx, sub] = full[ctx * per + sub]
    all_mixed = allm.reshape(sequence, channels)
    scale = 1.0 / math.sqrt(sequence)

    def weight(i):
        at = pl.ds(pl.multiple_of(i * LANES, LANES), LANES)
        left = all_mixed[:, at].T
        for sub in range(per):
            gw_ref[at, sub * width : (sub + 1) * width] = scale * jnp.dot(
                left, allg[:, sub].reshape(sequence, width), preferred_element_type=f32
            )

    loop(0, channels // LANES, weight)

    def gather_rs(d):
        rs_copy(d).wait_recv()
        mine[...] += rs_in[d].astype(f32)

    loop(1, chips, gather_rs)
    block_ref[...] = mine[...].astype(bf16)
    gt_ref[...] = taps_own[...]

    def gather_taps(d):
        tap_copy(d).wait_recv()
        gt_ref[...] += taps_in[d]

    loop(1, ctx_size, gather_taps)

    @pl.when(has_last)
    def _():
        halo_down.wait_send()

    def settle(d):
        ag_copy(d).wait_send()
        rs_copy(d).wait_send()

    loop(1, chips, settle)

    def settle_all(d):
        mate_copy(d).wait_send()
        pair_copy(d).wait_send()
        away, copy = a2_copy(d)

        @pl.when(away)
        def _():
            copy.wait_send()

    loop(0, chips, settle_all)

    def settle_ctx(d):
        mix_copy(d).wait_send()
        tap_copy(d).wait_send()

    loop(1, ctx_size, settle_ctx)
    each_chunk(True, lambda source, sub: relay_copy(source, sub).wait_send())


def local(projected, filters, out_weight, grad_out):
    _, rows, channels = projected.shape
    groups, taps_count = filters.shape
    group_size = channels // groups
    width = grad_out.shape[1]
    ctx_size, tp_size = lax.axis_size("ctx"), lax.axis_size("tp")
    chips, per = tp_size // 2, tp_size // ctx_size
    sequence = ctx_size * rows
    taps = filters.astype(jnp.bfloat16).astype(jnp.float32)
    zeros = jnp.zeros_like(taps)
    table_ahead = jnp.concatenate([taps, zeros], axis=1)
    table_back = jnp.concatenate([taps[:, ::-1], zeros], axis=1)
    f32, bf16 = jnp.float32, jnp.bfloat16
    dma = pltpu.SemaphoreType.DMA
    in_vmem = pl.BlockSpec(memory_space=pltpu.VMEM)
    block_out, grad_inputs, grad_weight, tap_grads = pl.pallas_call(
        functools.partial(whole_kernel, ctx_size, tp_size, group_size),
        in_specs=[in_vmem] * 5,
        out_specs=[in_vmem] * 4,
        out_shape=[
            jax.ShapeDtypeStruct((rows, width), bf16),
            jax.ShapeDtypeStruct((3, rows, channels), bf16),
            jax.ShapeDtypeStruct((channels, per * width), f32),
            jax.ShapeDtypeStruct((groups, taps_count), f32),
        ],
        scratch_shapes=[
            pltpu.VMEM((tp_size, rows, width), bf16),
            pltpu.VMEM((ctx_size, per, rows, width), bf16),
            pltpu.VMEM((ctx_size, rows, channels), bf16),
            pltpu.VMEM((taps_count, channels), bf16),
            pltpu.VMEM((taps_count, channels), bf16),
            pltpu.VMEM((rows, channels), f32),
            pltpu.VMEM((rows, channels), f32),
            pltpu.VMEM((rows, channels), bf16),
            pltpu.VMEM((chips, rows, width), bf16),
            pltpu.VMEM((chips, rows, width), bf16),
            pltpu.VMEM((rows, width), f32),
            pltpu.VMEM((chips, rows, width), bf16),
            pltpu.VMEM((chips, rows, width), bf16),
            pltpu.VMEM((groups, taps_count), f32),
            pltpu.VMEM((ctx_size, groups, taps_count), f32),
            dma((4,)),
            dma((chips,)), dma((chips,)),
            dma((chips,)), dma((chips,)),
            dma((chips,)), dma((ctx_size, per)),
            dma((ctx_size, per)), dma((ctx_size, per)),
            dma((ctx_size,)), dma((ctx_size,)),
            dma((chips,)), dma((chips,)),
            dma((chips,)), dma((chips,)),
            dma((ctx_size,)), dma((ctx_size,)),
        ],
        compiler_params=pltpu.CompilerParams(
            collective_id=0, has_side_effects=True, vmem_limit_bytes=56 * 1024 * 1024
        ),
    )(projected, table_back, table_ahead, out_weight, grad_out)
    own_taps = lax.dynamic_slice_in_dim(
        tap_grads[:, ::-1], lax.axis_index("ctx") * (taps_count // ctx_size),
        taps_count // ctx_size, 1,
    )
    return (block_out, grad_inputs, grad_weight, own_taps / math.sqrt(sequence * group_size))


def solution(mesh):
    placed = (P(None, "ctx", "tp"), P("tp", None), P("tp", None), P("ctx", "tp"))
    return jax.shard_map(
        local,
        mesh=mesh,
        in_specs=placed,
        out_specs=(P("ctx", "tp"), P(None, "ctx", "tp"), P("tp", "ctx"), P("tp", "ctx")),
        check_vma=False,
    )
```

time: 212 us -> 104 us (0.49)
  the two profiles are of different devices: /device:TPU:0 before, /device:TPU:12 now
where the time goes in v1:
time: 104 us; the launch traced here: 103 us
  Pallas kernels  90 us (87%)
  local copies, waits for them, and re-layouts  11.8 us (11%)
    pallas_call x1, Pallas kernels, local(): pl.pallas_call(functools.partial(whole_kernel, ctx_size, tp_size, group_s...  90 us
    unnamed x4, local copies, waits for them, and re-layouts  9.65 us

profile of v1, /device:TPU:12, one launch (start us, length us, event | category | flops | bytes accessed | tf_op | source)
XLA Modules:
  0.0 103.2 jit_solution(6527326300248772475)
XLA Ops:
  0.6 0.7 convert_convert_fusion
  1.4 0.1 rev.6
  1.5 0.6 concatenate.7.table_ahead
  2.1 0.6 concatenate.6.table_back
  2.7 90.0 %shard_map.75 = (bf16[256,768]{1,0:T(8,128)(2,1)}, bf16[3,256,768]{2,1,0:T(8,128)(2,1)}, f32[768,1536]{1,0:T(8,128)}, f32[48,128]{1,0:T(8,128)}) custom-call(bf16[3,256,768]{2,1,0:T(8,128)(2,1)} %p_ref.1, f32[48,256]{1,0:T(8,128)} %concatenate.6.table_back, f32[48,256]{1,0:T(8,128)} %concatenate.7.table_ahead, bf16[768,6144]{1,0:T(8,128)(2,1)} %w_ref.1, ...), custom_call_target="tpu_custom_call" | custom-call | tf_op jit(solution)/shard_map/pallas_call | solution.py:382
  92.7 0.8 rev.7
  93.5 0.1 dynamic-slice_multiply_fusion
  93.6 0.7 copy.8
  94.3 1.8 %copy.12 = bf16[256,768]{1,0:T(8,128)(2,1)} copy(bf16[256,768]{1,0:T(8,128)(2,1)} %get-tuple-element.20) | data formatting | bytes 786432
  96.0 2.4 %copy.13 = bf16[3,256,768]{2,1,0:T(8,128)(2,1)} copy(bf16[3,256,768]{2,1,0:T(8,128)(2,1)} %get-tuple-element.21) | data formatting | bytes 2359296
  98.4 4.8 %copy.14 = f32[768,1536]{1,0:T(8,128)} copy(f32[768,1536]{1,0:T(8,128)} %get-tuple-element.22) | data formatting | bytes 9437184

commit v2 on v1

--- a/solution.py
+++ b/solution.py
@@ -39,11 +39,11 @@
 
 
 def whole_kernel(
-    ctx_size, tp_size, group_size, p_ref, table_back, table_ahead, w_ref, go_ref,
-    block_ref, gi_ref, gw_ref, gt_ref,
-    full, allg, allm, halo, following, filtered, gm, gf, part_out, part_in, mine, rs_out, rs_in,
+    ctx_size, tp_size, group_size, p_ref, table_back, table_ahead, w_hbm, go_ref,
+    block_ref, gi_ref, allm, allg, gt_ref,
+    full, w_ref, halo, following, filtered, gm, gf, part_out, part_in, mine, rs_out, rs_in,
     taps_own, taps_in,
-    shift_sem, ag_send, ag_recv, mf_send, mf_recv, a2_send, a2_recv, am_send, am_recv,
+    w_sem, shift_sem, up_send, up_recv, down_send, down_recv, mf_send, mf_recv, a2_send, a2_recv, am_send, am_recv,
     mix_send, mix_recv, pm_send, pm_recv, rs_send, rs_recv, tap_send, tap_recv,
 ):
     chips = tp_size // 2
@@ -53,7 +53,6 @@
     taps_count = halo.shape[0]
     blocks = rows // taps_count
     tile_groups = LANES // group_size
-    sequence = ctx_size * rows
     ctx, tp = lax.axis_index("ctx"), lax.axis_index("tp")
     core, pos = lax.rem(tp, 2), lax.div(tp, 2)
     mate = tp + 1 - 2 * core
@@ -75,9 +74,6 @@
     def chip_after(d):
         return lax.rem(pos + d, chips) * 2 + core
 
-    def chip_before(d):
-        return lax.rem(pos - d + chips, chips) * 2 + core
-
     def ctx_after(d):
         return lax.rem(ctx + d, ctx_size)
 
@@ -87,33 +83,66 @@
     def lanes(i, size):
         return pl.ds(pl.multiple_of(i * size, LANES), size)
 
+    def chunk(sub):
+        return pl.ds(sub * width, width) if isinstance(sub, int) else lanes(sub, width)
+
     barrier = pltpu.get_barrier_semaphore()
 
     def greet(c, t):
         pl.semaphore_signal(barrier, inc=1, device_id=(c, t), device_id_type=pl.DeviceIdType.MESH)
 
+    weights = pltpu.make_async_copy(w_hbm, w_ref, w_sem.at[0])
+    weights.start()
     loop(1, chips, lambda d: greet(ctx, chip_after(d)))
     loop(1, ctx_size, lambda d: greet(ctx_after(d), tp))
     greet(ctx, mate)
     pl.semaphore_wait(barrier, chips + ctx_size - 1)
 
-    def ag_copy(d):
-        return remote(go_ref, full.at[tp], ag_send.at[d], ag_recv.at[d], ctx, chip_after(d))
-
-    def mate_copy(d):
-        k = chip_before(d)
-        return remote(full.at[k], full.at[k], mf_send.at[d], mf_recv.at[d], ctx, mate)
-
-    def a2_copy(d):
-        k = chip_before(d)
+    def up_copy(h):
+        k = tp - 2 * h
+        return remote(full.at[k], full.at[k], up_send.at[h], up_recv.at[h], ctx, tp + 2)
+
+    def up_landed(h):
+        k = tp - 2 * (h + 1)
+        return remote(full.at[k], full.at[k], up_send.at[h], up_recv.at[h], ctx, tp - 2)
+
+    def down_copy(h):
+        k = tp + 2 * h
+        return remote(full.at[k], full.at[k], down_send.at[h], down_recv.at[h], ctx, tp - 2)
+
+    def down_landed(h):
+        k = tp + 2 * (h + 1)
+        return remote(full.at[k], full.at[k], down_send.at[h], down_recv.at[h], ctx, tp + 2)
+
+    def sends_up(h):
+        return jnp.logical_and(pos - h >= 0, pos + 1 < chips)
+
+    def sends_down(h):
+        return jnp.logical_and(pos + h < chips, pos >= 1)
+
+    def pass_on(h):
+        @pl.when(sends_up(h))
+        def _():
+            up_copy(h).start()
+
+        @pl.when(sends_down(h))
+        def _():
+            down_copy(h).start()
+
+    def mate_copy(m):
+        k = 2 * m + core
+        return remote(full.at[k], full.at[k], mf_send.at[m], mf_recv.at[m], ctx, mate)
+
+    def a2_copy(m):
+        k = 2 * m + core
         owner, sub = lax.div(k, per), lax.rem(k, per)
         copy = remote(
-            full.at[k], allg.at[ctx, sub], a2_send.at[d], a2_recv.at[ctx, sub], owner, tp
+            full.at[k], allg.at[ctx, :, chunk(sub)], a2_send.at[m], a2_recv.at[ctx, sub], owner, tp
         )
         return owner != ctx, copy
 
-    def start_a2(d):
-        away, copy = a2_copy(d)
+    def start_a2(m):
+        away, copy = a2_copy(m)
 
         @pl.when(away)
         def _():
@@ -133,9 +162,32 @@
     def _():
         halo_up.start()
 
-    loop(1, chips, lambda d: ag_copy(d).start())
-    mate_copy(0).start()
-    start_a2(0)
+    pass_on(0)
+    mate_copy(pos).start()
+    start_a2(pos)
+
+    def arrive(h):
+        @pl.when(pos - 1 - h >= 0)
+        def _():
+            up_landed(h).wait_recv()
+
+            @pl.when(pos + 1 < chips)
+            def _():
+                up_copy(h + 1).start()
+
+            mate_copy(pos - 1 - h).start()
+            start_a2(pos - 1 - h)
+
+        @pl.when(pos + 1 + h < chips)
+        def _():
+            down_landed(h).wait_recv()
+
+            @pl.when(pos >= 1)
+            def _():
+                down_copy(h + 1).start()
+
+            mate_copy(pos + 1 + h).start()
+            start_a2(pos + 1 + h)
 
     @pl.when(has_last)
     def _():
@@ -173,7 +225,10 @@
             allm.at[ctx], allm.at[ctx], mix_send.at[d], mix_recv.at[d], ctx_after(d), tp
         )
 
+    first, second = min(1, chips - 1), min(2, chips - 1)
+    loop(0, first, arrive)
     loop(1, ctx_size, lambda d: mix_copy(d).start())
+    weights.wait()
 
     def pair_copy(m):
         return remote(part_out.at[m], part_in.at[m], pm_send.at[m], pm_recv.at[m], ctx, mate)
@@ -187,6 +242,7 @@
         pair_copy(m).start()
 
     loop(1, chips + 1, other_half)
+    loop(first, second, arrive)
 
     def rs_copy(d):
         return remote(rs_out.at[d], rs_in.at[d], rs_send.at[d], rs_recv.at[d], ctx, chip_after(d))
@@ -212,20 +268,27 @@
     gm[...] = jnp.zeros_like(gm)
     add_grad(tp)
 
-    def arrive(d):
-        ag_copy(d).wait_recv()
-        mate_copy(d).start()
-        start_a2(d)
-        add_grad(chip_before(d))
-
-    def arrive_mate(d):
-        mate_copy(d).wait_recv()
-        add_grad(chip_before(d) + 1 - 2 * core)
-
-    mate_first = 0
-    arrive_mate(mate_first)
-    loop(1, chips, arrive)
-    loop(1, chips, arrive_mate)
+    def add_mate(m):
+        mate_copy(m).wait_recv()
+        add_grad(2 * m + 1 - core)
+
+    def add_hop(h):
+        @pl.when(pos - 1 - h >= 0)
+        def _():
+            add_grad(tp - 2 * (h + 1))
+
+        @pl.when(pos + 1 + h < chips)
+        def _():
+            add_grad(tp + 2 * (h + 1))
+
+    def late_hop(h):
+        arrive(h)
+        add_hop(h)
+
+    add_mate(pos)
+    loop(0, second, add_hop)
+    loop(second, chips - 1, late_hop)
+    loop(1, chips, lambda d: add_mate(lax.rem(pos + d, chips)))
 
     gf[...] = (gm[...] * p_ref[0].astype(f32)).astype(bf16)
 
@@ -237,7 +300,7 @@
 
     def relay_copy(source, sub):
         return remote(
-            allg.at[source, sub], allg.at[source, sub], am_send.at[source, sub],
+            allg.at[source, :, chunk(sub)], allg.at[source, :, chunk(sub)], am_send.at[source, sub],
             am_recv.at[source, sub], ctx, mate,
         )
 
@@ -255,7 +318,7 @@
 
     def relay(source, sub):
         remote(
-            allg.at[source, sub], allg.at[source, sub], a2_send.at[0], a2_recv.at[source, sub], ctx, mate
+            allg.at[source, :, chunk(sub)], allg.at[source, :, chunk(sub)], a2_send.at[0], a2_recv.at[source, sub], ctx, mate
         ).wait_recv()
         relay_copy(source, sub).start()
 
@@ -307,19 +370,7 @@
     each_chunk(False, lambda source, sub: relay_copy(source, sub).wait_recv())
     loop(1, ctx_size, lambda d: mix_copy(d).wait_recv())
     for sub in range(per):
-        allg[ctx, sub] = full[ctx * per + sub]
-    all_mixed = allm.reshape(sequence, channels)
-    scale = 1.0 / math.sqrt(sequence)
-
-    def weight(i):
-        at = pl.ds(pl.multiple_of(i * LANES, LANES), LANES)
-        left = all_mixed[:, at].T
-        for sub in range(per):
-            gw_ref[at, sub * width : (sub + 1) * width] = scale * jnp.dot(
-                left, allg[:, sub].reshape(sequence, width), preferred_element_type=f32
-            )
-
-    loop(0, channels // LANES, weight)
+        allg[ctx, :, chunk(sub)] = full[ctx * per + sub]
 
     def gather_rs(d):
         rs_copy(d).wait_recv()
@@ -339,11 +390,18 @@
     def _():
         halo_down.wait_send()
 
-    def settle(d):
-        ag_copy(d).wait_send()
-        rs_copy(d).wait_send()
-
-    loop(1, chips, settle)
+    def settle(h):
+        rs_copy(h + 1).wait_send()
+
+        @pl.when(sends_up(h))
+        def _():
+            up_copy(h).wait_send()
+
+        @pl.when(sends_down(h))
+        def _():
+            down_copy(h).wait_send()
+
+    loop(0, chips - 1, settle)
 
     def settle_all(d):
         mate_copy(d).wait_send()
@@ -379,20 +437,20 @@
     f32, bf16 = jnp.float32, jnp.bfloat16
     dma = pltpu.SemaphoreType.DMA
     in_vmem = pl.BlockSpec(memory_space=pltpu.VMEM)
-    block_out, grad_inputs, grad_weight, tap_grads = pl.pallas_call(
+    block_out, grad_inputs, all_mixed, all_grad, tap_grads = pl.pallas_call(
         functools.partial(whole_kernel, ctx_size, tp_size, group_size),
-        in_specs=[in_vmem] * 5,
-        out_specs=[in_vmem] * 4,
+        in_specs=[in_vmem] * 3 + [pl.BlockSpec(memory_space=pl.ANY), in_vmem],
+        out_specs=[in_vmem] * 5,
         out_shape=[
             jax.ShapeDtypeStruct((rows, width), bf16),
             jax.ShapeDtypeStruct((3, rows, channels), bf16),
-            jax.ShapeDtypeStruct((channels, per * width), f32),
+            jax.ShapeDtypeStruct((ctx_size, rows, channels), bf16),
+            jax.ShapeDtypeStruct((ctx_size, rows, per * width), bf16),
             jax.ShapeDtypeStruct((groups, taps_count), f32),
         ],
         scratch_shapes=[
             pltpu.VMEM((tp_size, rows, width), bf16),
-            pltpu.VMEM((ctx_size, per, rows, width), bf16),
-            pltpu.VMEM((ctx_size, rows, channels), bf16),
+            pltpu.VMEM(out_weight.shape, bf16),
             pltpu.VMEM((taps_count, channels), bf16),
             pltpu.VMEM((taps_count, channels), bf16),
             pltpu.VMEM((rows, channels), f32),
@@ -405,7 +463,9 @@
             pltpu.VMEM((chips, rows, width), bf16),
             pltpu.VMEM((groups, taps_count), f32),
             pltpu.VMEM((ctx_size, groups, taps_count), f32),
+            dma((1,)),
             dma((4,)),
+            dma((chips,)), dma((chips,)),
             dma((chips,)), dma((chips,)),
             dma((chips,)), dma((chips,)),
             dma((chips,)), dma((ctx_size, per)),
@@ -419,6 +479,12 @@
             collective_id=0, has_side_effects=True, vmem_limit_bytes=56 * 1024 * 1024
         ),
     )(projected, table_back, table_ahead, out_weight, grad_out)
+    grad_weight = jnp.einsum(
+        "tc,td->cd",
+        all_mixed.reshape(sequence, channels),
+        all_grad.reshape(sequence, per * width),
+        preferred_element_type=f32,
+    ) * (1.0 / math.sqrt(sequence))
     own_taps = lax.dynamic_slice_in_dim(
         tap_grads[:, ::-1], lax.axis_index("ctx") * (taps_count // ctx_size),
         taps_count // ctx_size, 1,

time: 104 us -> 89.9 us (0.86)
  the two profiles are of different devices: /device:TPU:12 before, /device:TPU:0 now
where the time goes in v2:
time: 89.9 us; the launch traced here: 89.6 us
  Pallas kernels  76.2 us (85%)
  matrix products  7.31 us (8%)
  local copies, waits for them, and re-layouts  4.59 us (5%)
    pallas_call x1, Pallas kernels, local(): pl.pallas_call(functools.partial(whole_kernel, ctx_size, tp_size, group_s...  76.2 us
    dot_general x1, matrix products, local(): jnp.einsum('tc,td->cd', all_mixed.reshape(sequence, channels), all_grad.r...  7.31 us
    unnamed x7, local copies, waits for them, and re-layouts  2.45 us

profile of v2, /device:TPU:0, one launch (start us, length us, event | category | flops | bytes accessed | tf_op | source)
XLA Modules:
  0.0 89.6 jit_solution(1454835727114665663)
XLA Ops:
  0.6 0.7 convert_convert_fusion
  1.4 0.1 rev.6
  1.5 0.6 concatenate.7.table_ahead
  2.1 0.6 concatenate.6.table_back
  2.7 76.2 %shard_map.75 = (bf16[256,768]{1,0:T(8,128)(2,1)}, bf16[3,256,768]{2,1,0:T(8,128)(2,1)}, bf16[4,256,768]{2,1,0:T(8,128)(2,1)}, bf16[4,256,1536]{2,1,0:T(8,128)(2,1)}, f32[48,128]{1,0:T(8,128)}) custom-call(bf16[3,256,768]{2,1,0:T(8,128)(2,1)} %p_ref.1, f32[48,256]{1,0:T(8,128)} %concatenate.6.table_back, f32[48,256]{1,0:T(8,128)} %concatenate.7.table_ahead, ...), custom_call_target="tpu_custom_call" | custom-call | tf_op jit(solution)/shard_map/pallas_call | solution.py:440
  78.9 0.8 rev.7
  79.8 0.1 dynamic-slice_multiply_fusion
  79.8 0.7 copy.9
  80.5 0.0 copy-start.1
  80.5 0.0 copy-start
  80.5 7.3 %bitcast_multiply_fusion = f32[768,1536]{1,0:T(8,128)} fusion(bf16[4,256,768]{2,1,0:T(8,128)(2,1)} %get-tuple-element.11, bf16[4,256,1536]{2,1,0:T(8,128)(2,1)} %get-tuple-element.12), kind=kOutput, calls=%fused_computation | convolution fusion | flops 2417098752 | bytes 9437184 | tf_op jit(solution)/shard_map/tc,td->cd/dot_general | solution.py:482
  87.8 0.0 copy-done.1
  87.8 0.7 copy.13
  88.6 0.0 copy-done
  88.6 1.0 %copy.14 = bf16[3,256,768]{2,1,0:T(8,128)(2,1)} copy(bf16[3,256,768]{2,1,0:T(8,128)(2,1)S(1)} %copy-done) | data formatting | bytes 2359296
Async XLA Ops:
  80.5 7.3 %copy-start.1 = (bf16[256,768]{1,0:T(8,128)(2,1)S(1)}, bf16[256,768]{1,0:T(8,128)(2,1)}, u32[]{:S(2)}) copy-start(bf16[256,768]{1,0:T(8,128)(2,1)} %get-tuple-element.22) | copy-start | bytes 1179652
  80.5 8.1 %copy-start = (bf16[3,256,768]{2,1,0:T(8,128)(2,1)S(1)}, bf16[3,256,768]{2,1,0:T(8,128)(2,1)}, u32[]{:S(2)}) copy-start(bf16[3,256,768]{2,1,0:T(8,128)(2,1)} %get-tuple-element.23) | copy-start | bytes 3538948

commit v3 on v2

--- a/solution.py
+++ b/solution.py
@@ -41,10 +41,10 @@
 def whole_kernel(
     ctx_size, tp_size, group_size, p_ref, table_back, table_ahead, w_hbm, go_ref,
     block_ref, gi_ref, allm, allg, gt_ref,
-    full, w_ref, halo, following, filtered, gm, gf, part_out, part_in, mine, rs_out, rs_in,
+    full, w_ref, halo, following, filtered, gm, gf, part_out, part_in, sums, rs_out, rs_up, rs_down,
     taps_own, taps_in,
     w_sem, shift_sem, up_send, up_recv, down_send, down_recv, mf_send, mf_recv, a2_send, a2_recv, am_send, am_recv,
-    mix_send, mix_recv, pm_send, pm_recv, rs_send, rs_recv, tap_send, tap_recv,
+    mix_send, mix_recv, pm_send, pm_recv, rs_send, ru_recv, rd_recv, tap_send, tap_recv,
 ):
     chips = tp_size // 2
     per = tp_size // ctx_size
@@ -244,20 +244,80 @@
     loop(1, chips + 1, other_half)
     loop(first, second, arrive)
 
-    def rs_copy(d):
-        return remote(rs_out.at[d], rs_in.at[d], rs_send.at[d], rs_recv.at[d], ctx, chip_after(d))
-
-    def own_half(d):
-        k = chip_after(d)
-        part = partial(k)
-        pair_copy(lax.div(k, 2)).wait_recv()
-        rs_out[d] = (part + part_in[lax.div(k, 2)].astype(f32)).astype(bf16)
-        rs_copy(d).start()
-
-    loop(1, chips, own_half)
-    own_part = partial(tp)
-    pair_copy(pos).wait_recv()
-    mine[...] = own_part + part_in[pos].astype(f32)
+    def up_sum(m):
+        return remote(rs_out.at[m], rs_up.at[m], rs_send.at[m], ru_recv.at[m], ctx, tp + 2)
+
+    def down_sum(m):
+        return remote(rs_out.at[m], rs_down.at[m], rs_send.at[m], rd_recv.at[m], ctx, tp - 2)
+
+    def up_sum_landed(m):
+        remote(rs_out.at[m], rs_up.at[m], rs_send.at[m], ru_recv.at[m], ctx, tp - 2).wait_recv()
+        sums[m] += rs_up[m].astype(f32)
+
+    def down_sum_landed(m):
+        remote(rs_out.at[m], rs_down.at[m], rs_send.at[m], rd_recv.at[m], ctx, tp + 2).wait_recv()
+        sums[m] += rs_down[m].astype(f32)
+
+    def send_up(m):
+        rs_out[m] = sums[m].astype(bf16)
+        up_sum(m).start()
+
+    def send_down(m):
+        rs_out[m] = sums[m].astype(bf16)
+        down_sum(m).start()
+
+    def add_pair(m):
+        part = partial(2 * m + core)
+        pair_copy(m).wait_recv()
+        sums[m] = part + part_in[m].astype(f32)
+
+    def own_half(t):
+        m = jnp.where(pos == 0, chips - 1 - t, t)
+        add_pair(m)
+
+        @pl.when(jnp.logical_and(pos == 0, m > pos))
+        def _():
+            send_up(m)
+
+        @pl.when(jnp.logical_and(pos == chips - 1, m < pos))
+        def _():
+            send_down(m)
+
+    loop(0, chips, own_half)
+
+    def relay_up(m):
+        up_sum_landed(m)
+        send_up(m)
+
+    def relay_down(m):
+        down_sum_landed(m)
+        send_down(m)
+
+    def early_relay():
+        @pl.when(jnp.logical_and(pos == 1, chips - 1 > pos))
+        def _():
+            relay_up(chips - 1)
+
+        @pl.when(jnp.logical_and(pos == chips - 2, 0 < pos))
+        def _():
+            relay_down(0)
+
+    def relay_sums(t):
+        up, down = chips - 1 - t, t
+        done_up = jnp.logical_and(pos == 1, up == chips - 1)
+        done_down = jnp.logical_and(pos == chips - 2, down == 0)
+
+        @pl.when(jnp.logical_and(jnp.logical_and(pos > 0, up > pos), jnp.logical_not(done_up)))
+        def _():
+            relay_up(up)
+
+        @pl.when(
+            jnp.logical_and(
+                jnp.logical_and(pos < chips - 1, down < pos), jnp.logical_not(done_down)
+            )
+        )
+        def _():
+            relay_down(down)
 
     def add_grad(k):
         gm[...] += lax.dot_general(
@@ -290,6 +350,7 @@
     loop(second, chips - 1, late_hop)
     loop(1, chips, lambda d: add_mate(lax.rem(pos + d, chips)))
 
+    early_relay()
     gf[...] = (gm[...] * p_ref[0].astype(f32)).astype(bf16)
 
     @pl.when(has_last)
@@ -361,6 +422,7 @@
         taps_own[group_rows(i), :] = jnp.concatenate(found, axis=0)
 
     loop(0, channels // LANES, backward)
+    loop(0, chips - 1, relay_sums)
 
     def tap_copy(d):
         return remote(taps_own, taps_in.at[d], tap_send.at[d], tap_recv.at[d], ctx_after(d), tp)
@@ -372,12 +434,15 @@
     for sub in range(per):
         allg[ctx, :, chunk(sub)] = full[ctx * per + sub]
 
-    def gather_rs(d):
-        rs_copy(d).wait_recv()
-        mine[...] += rs_in[d].astype(f32)
-
-    loop(1, chips, gather_rs)
-    block_ref[...] = mine[...].astype(bf16)
+    @pl.when(pos > 0)
+    def _():
+        up_sum_landed(pos)
+
+    @pl.when(pos < chips - 1)
+    def _():
+        down_sum_landed(pos)
+
+    block_ref[...] = sums[pos].astype(bf16)
     gt_ref[...] = taps_own[...]
 
     def gather_taps(d):
@@ -391,7 +456,7 @@
         halo_down.wait_send()
 
     def settle(h):
-        rs_copy(h + 1).wait_send()
+        up_sum(lax.rem(pos + h + 1, chips)).wait_send()
 
         @pl.when(sends_up(h))
         def _():
@@ -458,7 +523,8 @@
             pltpu.VMEM((rows, channels), bf16),
             pltpu.VMEM((chips, rows, width), bf16),
             pltpu.VMEM((chips, rows, width), bf16),
-            pltpu.VMEM((rows, width), f32),
+            pltpu.VMEM((chips, rows, width), f32),
+            pltpu.VMEM((chips, rows, width), bf16),
             pltpu.VMEM((chips, rows, width), bf16),
             pltpu.VMEM((chips, rows, width), bf16),
             pltpu.VMEM((groups, taps_count), f32),
@@ -472,7 +538,7 @@
             dma((ctx_size, per)), dma((ctx_size, per)),
             dma((ctx_size,)), dma((ctx_size,)),
             dma((chips,)), dma((chips,)),
-            dma((chips,)), dma((chips,)),
+            dma((chips,)), dma((chips,)), dma((chips,)),
             dma((ctx_size,)), dma((ctx_size,)),
         ],
         compiler_params=pltpu.CompilerParams(

time: 89.9 us -> 87.2 us (0.970)
  Pallas kernels: 76.2 us -> 73.5 us
    pallas_call x1, Pallas kernels: 76.2 us -> 73.5 us  [local(): pl.pallas_call(functools.partial(whole_kernel, ctx_size, tp_size, group_s...]
where the time goes in v3:
time: 87.2 us; the launch traced here: 86.9 us
  Pallas kernels  73.5 us (84%)
  matrix products  7.31 us (8%)
  local copies, waits for them, and re-layouts  4.59 us (5%)
    pallas_call x1, Pallas kernels, local(): pl.pallas_call(functools.partial(whole_kernel, ctx_size, tp_size, group_s...  73.5 us
    dot_general x1, matrix products, local(): jnp.einsum('tc,td->cd', all_mixed.reshape(sequence, channels), all_grad.r...  7.31 us
    unnamed x7, local copies, waits for them, and re-layouts  2.45 us

profile of v3, /device:TPU:0, one launch (start us, length us, event | category | flops | bytes accessed | tf_op | source)
XLA Modules:
  0.0 86.9 jit_solution(3993357682969074901)
XLA Ops:
  0.6 0.7 convert_convert_fusion
  1.4 0.1 rev.6
  1.5 0.6 concatenate.7.table_ahead
  2.1 0.6 concatenate.6.table_back
  2.7 73.5 %shard_map.75 = (bf16[256,768]{1,0:T(8,128)(2,1)}, bf16[3,256,768]{2,1,0:T(8,128)(2,1)}, bf16[4,256,768]{2,1,0:T(8,128)(2,1)}, bf16[4,256,1536]{2,1,0:T(8,128)(2,1)}, f32[48,128]{1,0:T(8,128)}) custom-call(bf16[3,256,768]{2,1,0:T(8,128)(2,1)} %p_ref.1, f32[48,256]{1,0:T(8,128)} %concatenate.6.table_back, f32[48,256]{1,0:T(8,128)} %concatenate.7.table_ahead, ...), custom_call_target="tpu_custom_call" | custom-call | tf_op jit(solution)/shard_map/pallas_call | solution.py:505
  76.2 0.8 rev.7
  77.0 0.1 dynamic-slice_multiply_fusion
  77.1 0.7 copy.9
  77.8 0.0 copy-start.1
  77.8 0.0 copy-start
  77.8 7.3 %bitcast_multiply_fusion = f32[768,1536]{1,0:T(8,128)} fusion(bf16[4,256,768]{2,1,0:T(8,128)(2,1)} %get-tuple-element.11, bf16[4,256,1536]{2,1,0:T(8,128)(2,1)} %get-tuple-element.12), kind=kOutput, calls=%fused_computation | convolution fusion | flops 2417098752 | bytes 9437184 | tf_op jit(solution)/shard_map/tc,td->cd/dot_general | solution.py:548
  85.1 0.0 copy-done.1
  85.1 0.7 copy.13
  85.9 0.0 copy-done
  85.9 1.0 %copy.14 = bf16[3,256,768]{2,1,0:T(8,128)(2,1)} copy(bf16[3,256,768]{2,1,0:T(8,128)(2,1)S(1)} %copy-done) | data formatting | bytes 2359296
Async XLA Ops:
  77.8 7.3 %copy-start.1 = (bf16[256,768]{1,0:T(8,128)(2,1)S(1)}, bf16[256,768]{1,0:T(8,128)(2,1)}, u32[]{:S(2)}) copy-start(bf16[256,768]{1,0:T(8,128)(2,1)} %get-tuple-element.22) | copy-start | bytes 1179652
  77.8 8.1 %copy-start = (bf16[3,256,768]{2,1,0:T(8,128)(2,1)S(1)}, bf16[3,256,768]{2,1,0:T(8,128)(2,1)}, u32[]{:S(2)}) copy-start(bf16[3,256,768]{2,1,0:T(8,128)(2,1)} %get-tuple-element.23) | copy-start | bytes 3538948
